TPU v7x, 256 devices: a whole 4x4x8 slice. The times are simulated.
256 devices in a mesh: seq: 16 (over x, y), head: 16 (over z, core).
Axes of the slice: x: 4, y: 4, z: 8, core: 2. Of those that a mesh axis runs over, the one named last changes fastest.
Arguments:
- activations: bfloat16 [65536, 768], P(('seq', 'head')), may hold values from -6 to 6
- ln_gain: bfloat16 [768], replicated, may hold values from 0.099609375 to 1.8984375
- w_query: bfloat16 [768, 768], replicated
- w_key: bfloat16 [768, 768], replicated
- w_value: bfloat16 [768, 768], replicated, may hold values from -0.21875 to 0.21875
- w_gate: bfloat16 [768, 768], replicated, may hold values from -0.21875 to 0.21875
- w_out: bfloat16 [768, 768], replicated, may hold values from -0.21875 to 0.21875
- bias_tiles: bfloat16 [16, 16, 128, 256], P(None, 'head'), may hold values from -6 to 6
- crop_lengths: int32 [16], replicated, may hold values from 1 to 16384, 65536 in all
- tile_index: int32 [512], P('seq'), may hold values from 0 to 15
- d_out: bfloat16 [65536, 768], P(('seq', 'head')), may hold values from -6 to 6
Outputs:
- d_activations: bfloat16 [65536, 768], P(('seq', 'head'))
- d_bias: float32 [16, 16, 128, 256], P(None, 'head')
Inputs may be any that keep to these rules, and one draw needn't show every extreme that they name: crop_lengths sum to 65536; the longest crop is exactly 16384 rows.
All inputs are finite; a program needn't handle non-finite values.
Results may differ from a plain program's by a relative error of at most 0.039.
The roundings to bfloat16 on the way count: a program that leaves them out, or rounds other values in their place, can miss the bound.
Values may be sent and summed in bfloat16 or wider, within the bound.
A program may use at most 128 MiB of HBM per device.

v0:
```python
import math
import jax
import jax.numpy as jnp
from jax import lax
from jax.sharding import PartitionSpec as P

BLOCK = 128
eps = 1e-05


def passed_along(array, axis, by):
    length = lax.axis_size(axis)
    pairs = [(i, i + by) for i in range(length) if 0 <= i + by < length]
    return lax.ppermute(array, axis, pairs)


def norm_rows(activations, ln_gain):
    values = activations.astype(jnp.float32)
    centred = values - jnp.mean(values, axis=1, keepdims=True)
    inverse = lax.rsqrt(jnp.mean(centred * centred, axis=1, keepdims=True) + eps)
    scaled = centred * inverse
    normed = (scaled * ln_gain.astype(jnp.float32)[None, :]).astype(jnp.bfloat16)
    return (normed, scaled, inverse)


def norm_back(d_normed, scaled, inverse, ln_gain):
    d_scaled = d_normed * ln_gain.astype(jnp.float32)[None, :]
    centre = jnp.mean(d_scaled, axis=1, keepdims=True)
    along = jnp.mean(d_scaled * scaled, axis=1, keepdims=True)
    return (inverse * (d_scaled - centre - scaled * along)).astype(jnp.bfloat16)


def window_mask(first, blocks, crop_lengths):
    bounds = jnp.cumsum(crop_lengths)

    def crop_of(positions):
        return jnp.sum((bounds[None, :] <= positions[:, None]).astype(jnp.int32), axis=1)

    queries = first + jnp.arange(blocks * BLOCK, dtype=jnp.int32)
    starts = first + BLOCK * jnp.arange(blocks, dtype=jnp.int32) - BLOCK
    key_pos = starts[:, None] + jnp.arange(2 * BLOCK, dtype=jnp.int32)[None, :]
    query_crop = crop_of(queries).reshape(blocks, BLOCK)
    key_crop = crop_of(key_pos.reshape(-1)).reshape(blocks, 2 * BLOCK)
    return (key_pos >= 0)[:, None, :] & (query_crop[:, :, None] == key_crop[:, None, :])


def attention_pass(
    queries, keys, values, keys_before, values_before, grad_out, bias, allowed, heads_here
):
    rows, width = queries.shape
    blocks = rows // BLOCK
    size = width // heads_here
    scale = 1.0 / math.sqrt(size)

    def split(array):
        return array.reshape(blocks, BLOCK, heads_here, size)

    query_blocks = split(queries)
    key_blocks = split(keys)
    value_blocks = split(values)
    grad_blocks = split(grad_out)
    key_prev = jnp.concatenate(
        [keys_before.reshape(1, BLOCK, heads_here, size), key_blocks[:-1]], axis=0
    )
    value_prev = jnp.concatenate(
        [values_before.reshape(1, BLOCK, heads_here, size), value_blocks[:-1]], axis=0
    )
    key_window = jnp.concatenate([key_prev, key_blocks], axis=1)
    value_window = jnp.concatenate([value_prev, value_blocks], axis=1)
    mask = allowed[:, None, :, :]
    scores = (
        jnp.einsum("nihd,njhd->nhij", query_blocks, key_window, preferred_element_type=jnp.float32)
        * scale
        + bias
    )
    scores = jnp.where(mask, scores, -1e30)
    top = jnp.max(scores, axis=3, keepdims=True)
    weights = jnp.where(mask, jnp.exp(scores - top), 0.0)
    probs = weights / jnp.sum(weights, axis=3, keepdims=True)
    probs_low = probs.astype(jnp.bfloat16)
    attended = jnp.einsum(
        "nhij,njhd->nihd", probs_low, value_window, preferred_element_type=jnp.float32
    )
    attended = attended.astype(jnp.bfloat16).reshape(rows, width)
    d_probs = jnp.einsum(
        "nihd,njhd->nhij", grad_blocks, value_window, preferred_element_type=jnp.float32
    )
    d_scores = probs * (d_probs - jnp.sum(probs * d_probs, axis=3, keepdims=True))
    d_low = d_scores.astype(jnp.bfloat16)
    d_queries = (
        jnp.einsum("nhij,njhd->nihd", d_low, key_window, preferred_element_type=jnp.float32) * scale
    )
    d_queries = d_queries.astype(jnp.bfloat16).reshape(rows, width)
    d_key_window = (
        jnp.einsum("nhij,nihd->njhd", d_low, query_blocks, preferred_element_type=jnp.float32)
        * scale
    )
    d_value_window = jnp.einsum(
        "nhij,nihd->njhd", probs_low, grad_blocks, preferred_element_type=jnp.float32
    )
    empty = jnp.zeros((1, BLOCK, heads_here, size), jnp.float32)
    d_keys = d_key_window[:, BLOCK:] + jnp.concatenate([d_key_window[1:, :BLOCK], empty], axis=0)
    d_values = d_value_window[:, BLOCK:] + jnp.concatenate(
        [d_value_window[1:, :BLOCK], empty], axis=0
    )
    return (
        attended,
        d_queries,
        d_keys.reshape(rows, width),
        d_values.reshape(rows, width),
        d_key_window[0, :BLOCK].reshape(BLOCK, width),
        d_value_window[0, :BLOCK].reshape(BLOCK, width),
        d_scores,
    )


def back_product(gradient, weight):
    return lax.dot_general(
        gradient, weight, (((1,), (1,)), ((), ())), preferred_element_type=jnp.float32
    )


def shards(
    activations,
    ln_gain,
    w_query,
    w_key,
    w_value,
    w_gate,
    w_out,
    bias_tiles,
    crop_lengths,
    tile_index,
    d_out,
):
    heads_here = bias_tiles.shape[1]
    normed, scaled, inverse = norm_rows(activations, ln_gain)
    queries = jnp.dot(normed, w_query, preferred_element_type=jnp.float32).astype(jnp.bfloat16)
    keys = jnp.dot(normed, w_key, preferred_element_type=jnp.float32).astype(jnp.bfloat16)
    values = jnp.dot(normed, w_value, preferred_element_type=jnp.float32).astype(jnp.bfloat16)
    gate_input = jnp.dot(normed, w_gate, preferred_element_type=jnp.float32).astype(jnp.bfloat16)
    d_mixed = back_product(d_out, w_out).astype(jnp.bfloat16)
    head_q, head_k, head_v, head_gin, head_dmix = (
        lax.all_to_all(queries, "head", split_axis=1, concat_axis=0, tiled=True),
        lax.all_to_all(keys, "head", split_axis=1, concat_axis=0, tiled=True),
        lax.all_to_all(values, "head", split_axis=1, concat_axis=0, tiled=True),
        lax.all_to_all(gate_input, "head", split_axis=1, concat_axis=0, tiled=True),
        lax.all_to_all(d_mixed, "head", split_axis=1, concat_axis=0, tiled=True),
    )
    head_gate = jax.nn.sigmoid(head_gin.astype(jnp.float32))
    head_grad = (head_dmix.astype(jnp.float32) * head_gate).astype(jnp.bfloat16)
    group_rows = head_q.shape[0]
    blocks = group_rows // BLOCK
    first = lax.axis_index("seq") * group_rows
    allowed = window_mask(first, blocks, crop_lengths)
    picks = (
        tile_index[:, None] == jnp.arange(bias_tiles.shape[0], dtype=jnp.int32)[None, :]
    ).astype(jnp.bfloat16)
    bias = jnp.einsum("nt,thij->nhij", picks, bias_tiles, preferred_element_type=jnp.float32)
    keys_before, values_before = passed_along((head_k[-BLOCK:], head_v[-BLOCK:]), "seq", 1)
    attended, d_queries, d_keys, d_values, d_key_edge, d_value_edge, d_scores = attention_pass(
        head_q, head_k, head_v, keys_before, values_before, head_grad, bias, allowed, heads_here
    )
    key_after, value_after = (
        passed_along(d_key_edge.astype(jnp.bfloat16), "seq", -1).astype(d_key_edge.dtype),
        passed_along(d_value_edge.astype(jnp.bfloat16), "seq", -1).astype(d_value_edge.dtype),
    )
    d_keys = jnp.concatenate([d_keys[:-BLOCK], d_keys[-BLOCK:] + key_after], axis=0).astype(
        jnp.bfloat16
    )
    d_values = jnp.concatenate([d_values[:-BLOCK], d_values[-BLOCK:] + value_after], axis=0).astype(
        jnp.bfloat16
    )
    local_tiles = jnp.einsum(
        "nt,nhij->thij", picks.astype(jnp.float32), d_scores, precision=lax.Precision.HIGHEST
    )
    d_bias = lax.psum(local_tiles.astype(jnp.bfloat16), "seq").astype(jnp.float32)
    head_dgate = (
        head_dmix.astype(jnp.float32) * attended.astype(jnp.float32) * head_gate * (1.0 - head_gate)
    ).astype(jnp.bfloat16)
    row_dq, row_dk, row_dv, d_gate = (
        lax.all_to_all(d_queries, "head", split_axis=0, concat_axis=1, tiled=True),
        lax.all_to_all(d_keys, "head", split_axis=0, concat_axis=1, tiled=True),
        lax.all_to_all(d_values, "head", split_axis=0, concat_axis=1, tiled=True),
        lax.all_to_all(head_dgate, "head", split_axis=0, concat_axis=1, tiled=True),
    )
    d_normed = back_product(row_dq, w_query)
    d_normed = d_normed + back_product(row_dk, w_key)
    d_normed = d_normed + back_product(row_dv, w_value)
    d_normed = d_normed + back_product(d_gate, w_gate)
    d_activations = norm_back(d_normed, scaled, inverse, ln_gain)
    return (d_activations, d_bias)


def solution(mesh):
    return jax.shard_map(
        shards,
        mesh=mesh,
        in_specs=(
            P(("seq", "head"), None),
            P(),
            P(),
            P(),
            P(),
            P(),
            P(),
            P(None, "head", None, None),
            P(),
            P("seq"),
            P(("seq", "head"), None),
        ),
        out_specs=(P(("seq", "head"), None), P(None, "head", None, None)),
        check_vma=False,
    )
```

profile of v0, /device:TPU:32, one launch (start us, length us, event | category | flops | bytes accessed | tf_op | source)
XLA Modules:
  0.0 312.4 jit_solution(1983866665688578780)
XLA Ops:
  10.4 1.9 convolution_convert_fusion.4
  13.3 8.6 %all-to-all-start.1 = ((bf16[256,16,48]{0,2,1:T(8,128)(2,1)}), bf16[256,16,48]{0,2,1:T(8,128)(2,1)S(1)}, u32[]{:S(2)}, u32[]{:S(2)}) async-start(bf16[256,16,48]{0,2,1:T(8,128)(2,1)} %bitcast.6), calls=%async_computation.1 | async-start | bytes 786432 | tf_op jit(solution)/shard_map/all_to_all | solution.py:144
  23.3 10.4 %all-to-all-done.1 = bf16[256,16,48]{0,2,1:T(8,128)(2,1)S(1)} async-done(((bf16[256,16,48]{0,2,1:T(8,128)(2,1)}), bf16[256,16,48]{0,2,1:T(8,128)(2,1)S(1)}, u32[]{:S(2)}, u32[]{:S(2)}) %all-to-all-start.1) | async-done | bytes 393248 | tf_op jit(solution)/shard_map/all_to_all | solution.py:144
  33.8 5.5 %all-to-all-start.3 = ((bf16[256,16,48]{0,2,1:T(8,128)(2,1)}), bf16[256,16,48]{0,2,1:T(8,128)(2,1)S(1)}, u32[]{:S(2)}, u32[]{:S(2)}) async-start(bf16[256,16,48]{0,2,1:T(8,128)(2,1)} %bitcast.11), calls=%async_computation.3 | async-start | bytes 786432 | tf_op jit(solution)/shard_map/all_to_all | solution.py:147
  40.6 1.9 copy.112
  42.5 8.9 %all-to-all-done.3 = bf16[256,16,48]{0,2,1:T(8,128)(2,1)S(1)} async-done(((bf16[256,16,48]{0,2,1:T(8,128)(2,1)}), bf16[256,16,48]{0,2,1:T(8,128)(2,1)S(1)}, u32[]{:S(2)}, u32[]{:S(2)}) %all-to-all-start.3) | async-done | bytes 393248 | tf_op jit(solution)/shard_map/all_to_all | solution.py:147
  51.4 5.3 %all-to-all-start.4 = ((bf16[256,16,48]{0,2,1:T(8,128)(2,1)}), bf16[256,16,48]{0,2,1:T(8,128)(2,1)S(1)}, u32[]{:S(2)}, u32[]{:S(2)}) async-start(bf16[256,16,48]{0,2,1:T(8,128)(2,1)} %bitcast.13), calls=%async_computation.4 | async-start | bytes 786432 | tf_op jit(solution)/shard_map/all_to_all | solution.py:146
  59.5 9.4 %all-to-all-done.4 = bf16[256,16,48]{0,2,1:T(8,128)(2,1)S(1)} async-done(((bf16[256,16,48]{0,2,1:T(8,128)(2,1)}), bf16[256,16,48]{0,2,1:T(8,128)(2,1)S(1)}, u32[]{:S(2)}, u32[]{:S(2)}) %all-to-all-start.4) | async-done | bytes 393248 | tf_op jit(solution)/shard_map/all_to_all | solution.py:146
  68.8 5.3 %all-to-all-start = ((bf16[256,16,48]{0,2,1:T(8,128)(2,1)}), bf16[256,16,48]{0,2,1:T(8,128)(2,1)S(1)}, u32[]{:S(2)}, u32[]{:S(2)}) async-start(bf16[256,16,48]{0,2,1:T(8,128)(2,1)} %bitcast), calls=%async_computation | async-start | bytes 786432 | tf_op jit(solution)/shard_map/all_to_all | solution.py:145
  75.5 1.9 convolution_convert_fusion.3
  79.9 6.3 %all-to-all-done = bf16[256,16,48]{0,2,1:T(8,128)(2,1)S(1)} async-done(((bf16[256,16,48]{0,2,1:T(8,128)(2,1)}), bf16[256,16,48]{0,2,1:T(8,128)(2,1)S(1)}, u32[]{:S(2)}, u32[]{:S(2)}) %all-to-all-start) | async-done | bytes 393248 | tf_op jit(solution)/shard_map/all_to_all | solution.py:145
  86.2 5.3 %all-to-all-start.2 = ((bf16[256,16,48]{0,2,1:T(8,128)(2,1)}), bf16[256,16,48]{0,2,1:T(8,128)(2,1)S(1)}, u32[]{:S(2)}, u32[]{:S(2)}) async-start(bf16[256,16,48]{0,2,1:T(8,128)(2,1)} %bitcast.168), calls=%async_computation.2 | async-start | bytes 786432 | tf_op jit(solution)/shard_map/all_to_all | solution.py:148
  95.5 4.1 %fusion.16 = f32[32,128,256]{2,0,1:T(8,128)} fusion(bf16[16,128,256]{2,1,0:T(8,128)(2,1)} %bitcast.180, s32[32]{0:T(128)} %param.20), kind=kOutput, calls=%fused_computation.29 | convolution fusion | flops 33554944 | bytes 5243008 | tf_op jit(solution)/shard_map/nt,thij->nhij/dot_general | solution.py:159
  102.5 1.9 reshape.253
  107.0 4.1 %collective-permute-start.1 = (bf16[128,48]{0,1:T(8,128)(2,1)}, bf16[128,48]{0,1:T(8,128)(2,1)}, u32[]{:S(2)}, u32[]{:S(2)}) collective-permute-start(bf16[128,48]{0,1:T(8,128)(2,1)} %slice.78), channel_id=1, source_target_pairs={{0,16},{16,32},{32,48},{48,64},{64,80},{80,96},{96,112},{112,128},... | collective-permute-start | bytes 36872 | tf_op jit(solution)/shard_map/ppermute | solution.py:14
  111.1 3.5 %collective-permute-start = (bf16[128,48]{0,1:T(8,128)(2,1)S(1)}, bf16[128,48]{0,1:T(8,128)(2,1)}, u32[]{:S(2)}, u32[]{:S(2)}) collective-permute-start(bf16[128,48]{0,1:T(8,128)(2,1)S(1)} %slice.76), channel_id=1, source_target_pairs={{0,16},{16,32},{32,48},{48,64},{64,80},{80,96},{96,112},{112,128},... | collective-permute-start | bytes 36872 | tf_op jit(solution)/shard_map/ppermute | solution.py:14
  119.8 12.2 %fusion.67 = (f32[32,128]{1,0:T(8,128)S(1)}, f32[32,128,256]{2,1,0:T(8,128)}) fusion(s32[32,256]{1,0:T(8,128)} %eq.32, s32[32,128]{1,0:T(8,128)} %bitcast.184, pred[32,256]{1,0:T(8,128)(4,1)} %fusion.46, f32[32,128,256]{2,0,1:T(8,128)} %fusion.16, bf16[32,128,48]{1,0,2:T(8,128)(2,1)S(1)} %reshape.250, bf16[32,128,1,48]{1,3,0,2:T(8,128)(2,1)S(1)} %copy.101, ...), kind=kOutput, calls=%fused_computation.106 | convolution fusion | flops 113508608 | bytes 9641984 | tf_op jit(solution)/shard_map/sub | solution.py:78
  132.0 3.0 fusion.19
  135.6 2.6 multiply_reduce_fusion
  146.0 1.9 all_to_all.125
  149.7 7.2 %all-to-all-start.5 = ((bf16[16,256,48]{1,2,0:T(8,128)(2,1)}), bf16[16,256,48]{1,2,0:T(8,128)(2,1)}, u32[]{:S(2)}, u32[]{:S(2)}) async-start(bf16[16,256,48]{1,2,0:T(8,128)(2,1)} %copy.119), calls=%async_computation.5 | async-start | bytes 786432 | tf_op jit(solution)/shard_map/all_to_all | solution.py:182
  162.9 6.1 %all-to-all-done.5 = bf16[16,256,48]{1,2,0:T(8,128)(2,1)} async-done(((bf16[16,256,48]{1,2,0:T(8,128)(2,1)}), bf16[16,256,48]{1,2,0:T(8,128)(2,1)}, u32[]{:S(2)}, u32[]{:S(2)}) %all-to-all-start.5) | async-done | bytes 393248 | tf_op jit(solution)/shard_map/all_to_all | solution.py:182
  169.0 5.8 %all-to-all-start.7 = ((bf16[16,256,48]{1,2,0:T(8,128)(2,1)}), bf16[16,256,48]{1,2,0:T(8,128)(2,1)}, u32[]{:S(2)}, u32[]{:S(2)}) async-start(bf16[16,256,48]{1,2,0:T(8,128)(2,1)} %bitcast.169), calls=%async_computation.7 | async-start | bytes 786432 | tf_op jit(solution)/shard_map/all_to_all | solution.py:184
  177.9 9.1 %all-to-all-done.7 = bf16[16,256,48]{1,2,0:T(8,128)(2,1)} async-done(((bf16[16,256,48]{1,2,0:T(8,128)(2,1)}), bf16[16,256,48]{1,2,0:T(8,128)(2,1)}, u32[]{:S(2)}, u32[]{:S(2)}) %all-to-all-start.7) | async-done | bytes 393248 | tf_op jit(solution)/shard_map/all_to_all | solution.py:184
  187.0 5.7 %all-to-all-start.6 = ((bf16[16,256,48]{1,2,0:T(8,128)(2,1)}), bf16[16,256,48]{1,2,0:T(8,128)(2,1)}, u32[]{:S(2)}, u32[]{:S(2)}) async-start(bf16[16,256,48]{1,2,0:T(8,128)(2,1)} %bitcast.157), calls=%async_computation.6 | async-start | bytes 786432 | tf_op jit(solution)/shard_map/all_to_all | solution.py:183
  193.0 3.1 %fusion.15 = f32[32,128,1,48]{1,3,0,2:T(8,128)S(1)} fusion(bf16[32,128,1,48]{1,3,0,2:T(8,128)(2,1)S(1)} %copy-done.10, bf16[31,128,1,48]{1,3,0,2:T(8,128)(2,1)S(1)} %copy-done.16, bf16[1,128,1,48]{1,3,0,2:T(8,128)(2,1)} %bitcast.15, f32[32,128,256]{2,1,0:T(8,128)} %get-tuple-element.13, f32[32,128]{1,0:T(8,128)S(1)} %get-tuple-element.12), kind=kOutput, calls=%fused_computation.28 | convolution fusion | flops 105512960 | bytes 5783552 | tf_op jit(solution)/shard_map/nhij,njhd->nihd/dot_general | solution.py:81
  196.8 6.9 %fusion.7 = bf16[16,1,128,256]{3,0,2,1:T(8,128)(2,1)} fusion(f32[32,128,256]{2,1,0:T(8,128)} %copy-done.1, s32[32]{0:T(128)S(1)} %copy-done.25), kind=kOutput, calls=%fused_computation.12 | convolution fusion | flops 201851392 | bytes 5243008 | tf_op jit(solution)/shard_map/nt,nhij->thij/dot_general | solution.py:174
  205.0 7.4 %all-to-all-start.8 = ((bf16[16,256,48]{1,2,0:T(8,128)(2,1)}), bf16[16,256,48]{1,2,0:T(8,128)(2,1)S(1)}, u32[]{:S(2)}, u32[]{:S(2)}) async-start(bf16[16,256,48]{1,2,0:T(8,128)(2,1)} %fusion.38), calls=%async_computation.8 | async-start | bytes 786432 | tf_op jit(solution)/shard_map/all_to_all | solution.py:185
  212.4 1.9 fusion.70
  217.5 6.8 %all-to-all-done.8 = bf16[16,256,48]{1,2,0:T(8,128)(2,1)S(1)} async-done(((bf16[16,256,48]{1,2,0:T(8,128)(2,1)}), bf16[16,256,48]{1,2,0:T(8,128)(2,1)S(1)}, u32[]{:S(2)}, u32[]{:S(2)}) %all-to-all-start.8) | async-done | bytes 393248 | tf_op jit(solution)/shard_map/all_to_all | solution.py:185
  226.0 76.6 %all-reduce.4.cloned.1.call-done = bf16[16,1,128,256]{3,0,2,1:T(8,128)(2,1)} async-done(((bf16[16,1,128,256]{3,0,2,1:T(8,128)(2,1)}), bf16[16,1,128,256]{3,0,2,1:T(8,128)(2,1)}) %all-reduce.4.cloned.1.call-update) | async-done | bytes 1048592 | tf_op jit(solution)/shard_map/psum | solution.py:177
  302.7 2.9 copy.133
  (134 shorter events, 54.3 us)
Async XLA Ops:
  7.2 14.7 %copy-start = (bf16[768,768]{1,0:T(8,128)(2,1)S(1)}, bf16[768,768]{1,0:T(8,128)(2,1)}, u32[]{:S(2)}) copy-start(bf16[768,768]{1,0:T(8,128)(2,1)} %param.16) | copy-start | bytes 3538948
  8.4 48.3 %copy-start.17 = (f32[256]{0:T(256)}, f32[256]{0:T(256)S(1)}, u32[]{:S(2)}) copy-start(f32[256]{0:T(256)S(1)} %broadcast_multiply_fusion.2) | copy-start | bytes 3076
  9.7 12.2 %copy-start.2 = (bf16[256,768]{1,0:T(8,128)(2,1)S(1)}, bf16[256,768]{1,0:T(8,128)(2,1)}, u32[]{:S(2)}) copy-start(bf16[256,768]{1,0:T(8,128)(2,1)} %param.11) | copy-start | bytes 1179652
  9.7 47.0 %copy-start.21 = (f32[256]{0:T(256)}, f32[256]{0:T(256)S(1)}, u32[]{:S(2)}) copy-start(f32[256]{0:T(256)S(1)} %add_rsqrt_fusion) | copy-start | bytes 3076
  10.4 46.3 %copy-start.19 = (f32[768]{0:T(1024)}, f32[768]{0:T(1024)S(1)}, u32[]{:S(2)}) copy-start(f32[768]{0:T(1024)S(1)} %convert_element_type.142) | copy-start | bytes 9220
  13.3 20.5 %all-to-all-start.1 = ((bf16[256,16,48]{0,2,1:T(8,128)(2,1)}), bf16[256,16,48]{0,2,1:T(8,128)(2,1)S(1)}, u32[]{:S(2)}, u32[]{:S(2)}) async-start(bf16[256,16,48]{0,2,1:T(8,128)(2,1)} %bitcast.6), calls=%async_computation.1 | async-start | bytes 786432 | tf_op jit(solution)/shard_map/all_to_all | solution.py:144
  21.9 17.4 %copy-start.13 = (bf16[768,768]{1,0:T(8,128)(2,1)S(1)}, bf16[768,768]{1,0:T(8,128)(2,1)}, u32[]{:S(2)}) copy-start(bf16[768,768]{1,0:T(8,128)(2,1)} %param.15) | copy-start | bytes 3538948
  33.8 17.6 %all-to-all-start.3 = ((bf16[256,16,48]{0,2,1:T(8,128)(2,1)}), bf16[256,16,48]{0,2,1:T(8,128)(2,1)S(1)}, u32[]{:S(2)}, u32[]{:S(2)}) async-start(bf16[256,16,48]{0,2,1:T(8,128)(2,1)} %bitcast.11), calls=%async_computation.3 | async-start | bytes 786432 | tf_op jit(solution)/shard_map/all_to_all | solution.py:147
  51.4 17.4 %all-to-all-start.4 = ((bf16[256,16,48]{0,2,1:T(8,128)(2,1)}), bf16[256,16,48]{0,2,1:T(8,128)(2,1)S(1)}, u32[]{:S(2)}, u32[]{:S(2)}) async-start(bf16[256,16,48]{0,2,1:T(8,128)(2,1)} %bitcast.13), calls=%async_computation.4 | async-start | bytes 786432 | tf_op jit(solution)/shard_map/all_to_all | solution.py:146
  56.7 17.4 %copy-start.26 = (s32[16]{0:T(128)S(1)}, s32[16]{0:T(128)}, u32[]{:S(2)}) copy-start(s32[16]{0:T(128)} %param.19) | copy-start | bytes 196
  68.8 17.4 %all-to-all-start = ((bf16[256,16,48]{0,2,1:T(8,128)(2,1)}), bf16[256,16,48]{0,2,1:T(8,128)(2,1)S(1)}, u32[]{:S(2)}, u32[]{:S(2)}) async-start(bf16[256,16,48]{0,2,1:T(8,128)(2,1)} %bitcast), calls=%async_computation | async-start | bytes 786432 | tf_op jit(solution)/shard_map/all_to_all | solution.py:145
  74.4 11.9 %copy-start.23 = (s32[16]{0:T(128)}, s32[16]{0:T(128)S(1)}, u32[]{:S(2)}) copy-start(s32[16]{0:T(128)S(1)} %reduce.6) | copy-start | bytes 196
  86.2 28.3 %all-to-all-start.2 = ((bf16[256,16,48]{0,2,1:T(8,128)(2,1)}), bf16[256,16,48]{0,2,1:T(8,128)(2,1)S(1)}, u32[]{:S(2)}, u32[]{:S(2)}) async-start(bf16[256,16,48]{0,2,1:T(8,128)(2,1)} %bitcast.168), calls=%async_computation.2 | async-start | bytes 786432 | tf_op jit(solution)/shard_map/all_to_all | solution.py:148
  101.6 18.2 %copy-start.6 = (bf16[32,128,48]{1,0,2:T(8,128)(2,1)}, bf16[32,128,48]{1,0,2:T(8,128)(2,1)S(1)}, u32[]{:S(2)}) copy-start(bf16[32,128,48]{1,0,2:T(8,128)(2,1)S(1)} %reshape.250) | copy-start | bytes 1179652
  105.5 5.6 %copy-start.8 = (bf16[32,128,1,48]{1,3,0,2:T(8,128)(2,1)}, bf16[32,128,1,48]{1,3,0,2:T(8,128)(2,1)S(1)}, u32[]{:S(2)}) copy-start(bf16[32,128,1,48]{1,3,0,2:T(8,128)(2,1)S(1)} %copy.115) | copy-start | bytes 1179652
  107.0 28.1 %collective-permute-start.1 = (bf16[128,48]{0,1:T(8,128)(2,1)}, bf16[128,48]{0,1:T(8,128)(2,1)}, u32[]{:S(2)}, u32[]{:S(2)}) collective-permute-start(bf16[128,48]{0,1:T(8,128)(2,1)} %slice.78), channel_id=1, source_target_pairs={{0,16},{16,32},{32,48},{48,64},{64,80},{80,96},{96,112},{112,128},... | collective-permute-start | bytes 36872 | tf_op jit(solution)/shard_map/ppermute | solution.py:14
  111.1 8.7 %collective-permute-start = (bf16[128,48]{0,1:T(8,128)(2,1)S(1)}, bf16[128,48]{0,1:T(8,128)(2,1)}, u32[]{:S(2)}, u32[]{:S(2)}) collective-permute-start(bf16[128,48]{0,1:T(8,128)(2,1)S(1)} %slice.76), channel_id=1, source_target_pairs={{0,16},{16,32},{32,48},{48,64},{64,80},{80,96},{96,112},{112,128},... | collective-permute-start | bytes 36872 | tf_op jit(solution)/shard_map/ppermute | solution.py:14
  114.6 3.9 %copy-start.4 = (bf16[256,16,48]{0,2,1:T(8,128)(2,1)}, bf16[256,16,48]{0,2,1:T(8,128)(2,1)S(1)}, u32[]{:S(2)}) copy-start(bf16[256,16,48]{0,2,1:T(8,128)(2,1)S(1)} %all-to-all-done.2) | copy-start | bytes 1179652
  142.8 18.6 %collective-permute-start.3 = (bf16[128,48]{0,1:T(8,128)(2,1)}, bf16[128,48]{0,1:T(8,128)(2,1)}, u32[]{:S(2)}, u32[]{:S(2)}) collective-permute-start(bf16[128,48]{0,1:T(8,128)(2,1)} %fusion.52), channel_id=1, source_target_pairs={{16,0},{32,16},{48,32},{64,48},{80,64},{96,80},{112,96},{128,112},... | collective-permute-start | bytes 36872 | tf_op jit(solution)/shard_map/ppermute | solution.py:14
  149.7 19.2 %all-to-all-start.5 = ((bf16[16,256,48]{1,2,0:T(8,128)(2,1)}), bf16[16,256,48]{1,2,0:T(8,128)(2,1)}, u32[]{:S(2)}, u32[]{:S(2)}) async-start(bf16[16,256,48]{1,2,0:T(8,128)(2,1)} %copy.119), calls=%async_computation.5 | async-start | bytes 786432 | tf_op jit(solution)/shard_map/all_to_all | solution.py:182
  159.0 17.4 %collective-permute-start.2 = (bf16[128,48]{0,1:T(8,128)(2,1)}, bf16[128,48]{0,1:T(8,128)(2,1)}, u32[]{:S(2)}, u32[]{:S(2)}) collective-permute-start(bf16[128,48]{0,1:T(8,128)(2,1)} %fusion.51), channel_id=1, source_target_pairs={{16,0},{32,16},{48,32},{64,48},{80,64},{96,80},{112,96},{128,112},... | collective-permute-start | bytes 36872 | tf_op jit(solution)/shard_map/ppermute | solution.py:14
  169.0 18.1 %all-to-all-start.7 = ((bf16[16,256,48]{1,2,0:T(8,128)(2,1)}), bf16[16,256,48]{1,2,0:T(8,128)(2,1)}, u32[]{:S(2)}, u32[]{:S(2)}) async-start(bf16[16,256,48]{1,2,0:T(8,128)(2,1)} %bitcast.169), calls=%async_computation.7 | async-start | bytes 786432 | tf_op jit(solution)/shard_map/all_to_all | solution.py:184
  176.1 16.9 %copy-start.10 = (bf16[32,128,1,48]{1,3,0,2:T(8,128)(2,1)S(1)}, bf16[32,128,1,48]{1,3,0,2:T(8,128)(2,1)}, u32[]{:S(2)}) copy-start(bf16[32,128,1,48]{1,3,0,2:T(8,128)(2,1)} %copy-done.8) | copy-start | bytes 1179652
  176.1 16.9 %copy-start.16 = (bf16[31,128,1,48]{1,3,0,2:T(8,128)(2,1)S(1)}, bf16[31,128,1,48]{1,3,0,2:T(8,128)(2,1)}, u32[]{:S(2)}) copy-start(bf16[31,128,1,48]{1,3,0,2:T(8,128)(2,1)} %slice.79) | copy-start | bytes 1142788
  187.0 18.0 %all-to-all-start.6 = ((bf16[16,256,48]{1,2,0:T(8,128)(2,1)}), bf16[16,256,48]{1,2,0:T(8,128)(2,1)}, u32[]{:S(2)}, u32[]{:S(2)}) async-start(bf16[16,256,48]{1,2,0:T(8,128)(2,1)} %bitcast.157), calls=%async_computation.6 | async-start | bytes 786432 | tf_op jit(solution)/shard_map/all_to_all | solution.py:183
  192.7 110.0 %all-reduce.4.cloned.1.call-start = ((), (), s32[]{:S(2)}) async-start(), calls=%async_computation.9 | async-start | bytes 2097152 | tf_op jit(solution)/shard_map/psum | solution.py:177
  196.8 6.9 %copy-start.5 = (bf16[256,16,48]{0,2,1:T(8,128)(2,1)S(1)}, bf16[256,16,48]{0,2,1:T(8,128)(2,1)}, u32[]{:S(2)}) copy-start(bf16[256,16,48]{0,2,1:T(8,128)(2,1)} %copy-done.4) | copy-start | bytes 1179652
  205.0 9.3 %copy-start.12 = (bf16[768,768]{1,0:T(8,128)(2,1)S(1)}, bf16[768,768]{1,0:T(8,128)(2,1)}, u32[]{:S(2)}) copy-start(bf16[768,768]{1,0:T(8,128)(2,1)} %param.14) | copy-start | bytes 3538948
  205.0 19.3 %all-to-all-start.8 = ((bf16[16,256,48]{1,2,0:T(8,128)(2,1)}), bf16[16,256,48]{1,2,0:T(8,128)(2,1)S(1)}, u32[]{:S(2)}, u32[]{:S(2)}) async-start(bf16[16,256,48]{1,2,0:T(8,128)(2,1)} %fusion.38), calls=%async_computation.8 | async-start | bytes 786432 | tf_op jit(solution)/shard_map/all_to_all | solution.py:185
  216.0 8.3 %copy-start.18 = (f32[256]{0:T(256)S(1)}, f32[256]{0:T(256)}, u32[]{:S(2)}) copy-start(f32[256]{0:T(256)} %copy-done.17) | copy-start | bytes 3076
  216.0 8.3 %copy-start.20 = (f32[768]{0:T(1024)S(1)}, f32[768]{0:T(1024)}, u32[]{:S(2)}) copy-start(f32[768]{0:T(1024)} %copy-done.19) | copy-start | bytes 9220
  216.0 8.3 %copy-start.22 = (f32[256]{0:T(256)S(1)}, f32[256]{0:T(256)}, u32[]{:S(2)}) copy-start(f32[256]{0:T(256)} %copy-done.21) | copy-start | bytes 3076
  (9 other events, 18.8 us)
Sparse Core Ops, SparseCore 0:
  203.8 98.8 all-reduce.3
where the time goes:
time: 315 us; the launch traced here: 312 us
  waiting for transfers between devices  134 us (43%)
  starting transfers between devices  66.5 us (21%)
  matrix products  47.2 us (15%)
  local copies, waits for them, and re-layouts  34.3 us (11%)
  other arithmetic  16.1 us (5%)
  between operations  14.6 us (5%)
    psum x1, waiting for transfers between devices, shards(): lax.psum(local_tiles.astype(jnp.bfloat16), 'seq').astype(jnp.float32)  76.6 us
    sub x1, matrix products, attention_pass(): weights = jnp.where(mask, jnp.exp(scores - top), 0.0)  12.2 us
    all_to_all x1, waiting for transfers between devices, shards(): lax.all_to_all(queries, 'head', split_axis=1, concat_axis=0, tiled=True)  10.4 us
    ppermute x4, starting transfers between devices, passed_along(): return lax.ppermute(array, axis, pairs)  10.1 us
    all_to_all x1, waiting for transfers between devices, shards(): lax.all_to_all(values, 'head', split_axis=1, concat_axis=0, tiled=True)  9.37 us
    all_to_all x1, waiting for transfers between devices, shards(): lax.all_to_all(d_values, 'head', split_axis=0, concat_axis=1, tiled=True)  9.12 us
    all_to_all x1, waiting for transfers between devices, shards(): lax.all_to_all(gate_input, 'head', split_axis=1, concat_axis=0, tiled=True)  8.9 us
    all_to_all x1, starting transfers between devices, shards(): lax.all_to_all(queries, 'head', split_axis=1, concat_axis=0, tiled=True)  8.59 us
  transfers between devices with their start and end apart: 14, of which 8 were waited for; matrix products, arithmetic and copies ran while one was open for 25% of the time, Pallas kernels for 0%

commit v1 on v0

--- a/solution.py
+++ b/solution.py
@@ -174,7 +174,9 @@
     local_tiles = jnp.einsum(
         "nt,nhij->thij", picks.astype(jnp.float32), d_scores, precision=lax.Precision.HIGHEST
     )
-    d_bias = lax.psum(local_tiles.astype(jnp.bfloat16), "seq").astype(jnp.float32)
+    d_bias = jnp.sum(jax.lax.all_gather(local_tiles.astype(jnp.bfloat16), "seq"), axis=0).astype(
+        jnp.float32
+    )
     head_dgate = (
         head_dmix.astype(jnp.float32) * attended.astype(jnp.float32) * head_gate * (1.0 - head_gate)
     ).astype(jnp.bfloat16)

time: 315 us -> 290 us (0.921)
  waiting for transfers between devices: 134 us -> 105 us
  other arithmetic: 16.1 us -> 26.7 us
  local copies, waits for them, and re-layouts: 34.3 us -> 29.7 us
    psum x1 -> x0, waiting for transfers between devices: 76.6 us -> none  [shards(): lax.psum(local_tiles.astype(jnp.bfloat16), 'seq').astype(jnp.float32)]
    all_gather x0 -> x1, waiting for transfers between devices: none -> 44.8 us  [shards(): jax.lax.all_gather(local_tiles.astype(jnp.bfloat16), 'seq')]
    all_to_all x1, waiting for transfers between devices: 9.37 us -> 0.01 us  [shards(): lax.all_to_all(values, 'head', split_axis=1, concat_axis=0, tiled=True)]
    reduce_sum x0 -> x1, other arithmetic: none -> 8.84 us  [shards(): jnp.sum(jax.lax.all_gather(local_tiles.astype(jnp.bfloat16), 'seq'), axis=0)]
    all_to_all x1, waiting for transfers between devices: 0.01 us -> 5.6 us  [shards(): lax.all_to_all(d_mixed, 'head', split_axis=1, concat_axis=0, tiled=True)]
    all_to_all x1, waiting for transfers between devices: 0.01 us -> 4.98 us  [shards(): lax.all_to_all(d_keys, 'head', split_axis=0, concat_axis=1, tiled=True)]
    all_to_all x1, waiting for transfers between devices: 6.34 us -> 10.4 us  [shards(): lax.all_to_all(keys, 'head', split_axis=1, concat_axis=0, tiled=True)]
    all_to_all x1, starting transfers between devices: 5.28 us -> 8.59 us  [shards(): lax.all_to_all(keys, 'head', split_axis=1, concat_axis=0, tiled=True)]
  transfers between devices with their start and end apart: 14 -> 14, of which waited for: 8 -> 9; matrix products, arithmetic and copies ran while one was open for 25% -> 25% of each run, Pallas kernels for 0% -> 0%
where the time goes in v1:
time: 290 us; the launch traced here: 288 us
  waiting for transfers between devices  105 us (36%)
  starting transfers between devices  64 us (22%)
  matrix products  47.2 us (16%)
  local copies, waits for them, and re-layouts  29.7 us (10%)
  other arithmetic  26.7 us (9%)
  between operations  14.6 us (5%)
    all_gather x1, waiting for transfers between devices, shards(): jax.lax.all_gather(local_tiles.astype(jnp.bfloat16), 'seq')  44.8 us
    sub x1, matrix products, attention_pass(): weights = jnp.where(mask, jnp.exp(scores - top), 0.0)  12.2 us
    all_to_all x1, waiting for transfers between devices, shards(): lax.all_to_all(queries, 'head', split_axis=1, concat_axis=0, tiled=True)  10.6 us
    all_to_all x1, waiting for transfers between devices, shards(): lax.all_to_all(keys, 'head', split_axis=1, concat_axis=0, tiled=True)  10.4 us
    ppermute x4, starting transfers between devices, passed_along(): return lax.ppermute(array, axis, pairs)  10.1 us
    all_to_all x1, waiting for transfers between devices, shards(): lax.all_to_all(gate_input, 'head', split_axis=1, concat_axis=0, tiled=True)  9.42 us
    all_to_all x1, waiting for transfers between devices, shards(): lax.all_to_all(d_values, 'head', split_axis=0, concat_axis=1, tiled=True)  9.08 us
    reduce_sum x1, other arithmetic, shards(): jnp.sum(jax.lax.all_gather(local_tiles.astype(jnp.bfloat16), 'seq'), axis=0)  8.84 us
  transfers between devices with their start and end apart: 14, of which 9 were waited for; matrix products, arithmetic and copies ran while one was open for 25% of the time, Pallas kernels for 0%

profile of v1, /device:TPU:32, one launch (start us, length us, event | category | flops | bytes accessed | tf_op | source)
XLA Modules:
  0.0 287.7 jit_solution(6090530497361979526)
XLA Ops:
  13.4 8.6 %all-to-all-start = ((bf16[256,16,48]{0,2,1:T(8,128)(2,1)}), bf16[256,16,48]{0,2,1:T(8,128)(2,1)S(1)}, u32[]{:S(2)}, u32[]{:S(2)}) async-start(bf16[256,16,48]{0,2,1:T(8,128)(2,1)} %bitcast), calls=%async_computation | async-start | bytes 786432 | tf_op jit(solution)/shard_map/all_to_all | solution.py:145
  23.4 10.4 %all-to-all-done = bf16[256,16,48]{0,2,1:T(8,128)(2,1)S(1)} async-done(((bf16[256,16,48]{0,2,1:T(8,128)(2,1)}), bf16[256,16,48]{0,2,1:T(8,128)(2,1)S(1)}, u32[]{:S(2)}, u32[]{:S(2)}) %all-to-all-start) | async-done | bytes 393248 | tf_op jit(solution)/shard_map/all_to_all | solution.py:145
  33.8 5.5 %all-to-all-start.1 = ((bf16[256,16,48]{0,2,1:T(8,128)(2,1)}), bf16[256,16,48]{0,2,1:T(8,128)(2,1)S(1)}, u32[]{:S(2)}, u32[]{:S(2)}) async-start(bf16[256,16,48]{0,2,1:T(8,128)(2,1)} %bitcast.6), calls=%async_computation.1 | async-start | bytes 786432 | tf_op jit(solution)/shard_map/all_to_all | solution.py:144
  40.8 10.6 %all-to-all-done.1 = bf16[256,16,48]{0,2,1:T(8,128)(2,1)S(1)} async-done(((bf16[256,16,48]{0,2,1:T(8,128)(2,1)}), bf16[256,16,48]{0,2,1:T(8,128)(2,1)S(1)}, u32[]{:S(2)}, u32[]{:S(2)}) %all-to-all-start.1) | async-done | bytes 393248 | tf_op jit(solution)/shard_map/all_to_all | solution.py:144
  51.5 5.4 %all-to-all-start.3 = ((bf16[256,16,48]{0,2,1:T(8,128)(2,1)}), bf16[256,16,48]{0,2,1:T(8,128)(2,1)S(1)}, u32[]{:S(2)}, u32[]{:S(2)}) async-start(bf16[256,16,48]{0,2,1:T(8,128)(2,1)} %bitcast.11), calls=%async_computation.3 | async-start | bytes 786432 | tf_op jit(solution)/shard_map/all_to_all | solution.py:147
  59.6 9.4 %all-to-all-done.3 = bf16[256,16,48]{0,2,1:T(8,128)(2,1)S(1)} async-done(((bf16[256,16,48]{0,2,1:T(8,128)(2,1)}), bf16[256,16,48]{0,2,1:T(8,128)(2,1)S(1)}, u32[]{:S(2)}, u32[]{:S(2)}) %all-to-all-start.3) | async-done | bytes 393248 | tf_op jit(solution)/shard_map/all_to_all | solution.py:147
  69.0 5.3 %all-to-all-start.2 = ((bf16[256,16,48]{0,2,1:T(8,128)(2,1)}), bf16[256,16,48]{0,2,1:T(8,128)(2,1)S(1)}, u32[]{:S(2)}, u32[]{:S(2)}) async-start(bf16[256,16,48]{0,2,1:T(8,128)(2,1)} %bitcast.10), calls=%async_computation.2 | async-start | bytes 786432 | tf_op jit(solution)/shard_map/all_to_all | solution.py:148
  80.9 5.6 %all-to-all-done.2 = bf16[256,16,48]{0,2,1:T(8,128)(2,1)S(1)} async-done(((bf16[256,16,48]{0,2,1:T(8,128)(2,1)}), bf16[256,16,48]{0,2,1:T(8,128)(2,1)S(1)}, u32[]{:S(2)}, u32[]{:S(2)}) %all-to-all-start.2) | async-done | bytes 393248 | tf_op jit(solution)/shard_map/all_to_all | solution.py:148
  86.5 5.3 %all-to-all-start.4 = ((bf16[256,16,48]{0,2,1:T(8,128)(2,1)}), bf16[256,16,48]{0,2,1:T(8,128)(2,1)S(1)}, u32[]{:S(2)}, u32[]{:S(2)}) async-start(bf16[256,16,48]{0,2,1:T(8,128)(2,1)} %bitcast.171), calls=%async_computation.4 | async-start | bytes 786432 | tf_op jit(solution)/shard_map/all_to_all | solution.py:146
  94.5 4.0 %fusion.13 = f32[32,128,256]{2,0,1:T(8,128)} fusion(bf16[16,128,256]{2,1,0:T(8,128)(2,1)} %bitcast.184, s32[32]{0:T(128)} %param.20), kind=kOutput, calls=%fused_computation.29 | convolution fusion | flops 33554944 | bytes 5243008 | tf_op jit(solution)/shard_map/nt,thij->nhij/dot_general | solution.py:159
  98.6 4.1 %collective-permute-start = (bf16[128,48]{0,1:T(8,128)(2,1)S(1)}, bf16[128,48]{0,1:T(8,128)(2,1)}, u32[]{:S(2)}, u32[]{:S(2)}) collective-permute-start(bf16[128,48]{0,1:T(8,128)(2,1)S(1)} %slice.76), channel_id=1, source_target_pairs={{0,16},{16,32},{32,48},{48,64},{64,80},{80,96},{96,112},{112,128},... | collective-permute-start | bytes 36872 | tf_op jit(solution)/shard_map/ppermute | solution.py:14
  114.4 3.5 %collective-permute-start.1 = (bf16[128,48]{0,1:T(8,128)(2,1)}, bf16[128,48]{0,1:T(8,128)(2,1)}, u32[]{:S(2)}, u32[]{:S(2)}) collective-permute-start(bf16[128,48]{0,1:T(8,128)(2,1)} %slice.78), channel_id=1, source_target_pairs={{0,16},{16,32},{32,48},{48,64},{64,80},{80,96},{96,112},{112,128},... | collective-permute-start | bytes 36872 | tf_op jit(solution)/shard_map/ppermute | solution.py:14
  117.9 12.2 %fusion.64 = (f32[32,128]{1,0:T(8,128)S(1)}, f32[32,128,256]{2,1,0:T(8,128)}) fusion(s32[32,256]{1,0:T(8,128)} %eq.32, s32[32,128]{1,0:T(8,128)} %bitcast.188, pred[32,256]{1,0:T(8,128)(4,1)} %fusion.43, f32[32,128,256]{2,0,1:T(8,128)} %fusion.13, bf16[32,128,48]{1,0,2:T(8,128)(2,1)S(1)} %reshape.262, bf16[32,128,1,48]{1,3,0,2:T(8,128)(2,1)S(1)} %copy.99, ...), kind=kOutput, calls=%fused_computation.106 | convolution fusion | flops 113508608 | bytes 9641984 | tf_op jit(solution)/shard_map/sub | solution.py:78
  130.1 4.1 %multiply_reduce_fusion = (f32[32,128]{1,0:T(8,128)S(1)}, f32[32,128,256]{2,1,0:T(8,128)S(1)}) fusion(f32[32,128,256]{2,1,0:T(8,128)} %get-tuple-element.9, f32[32,128]{1,0:T(8,128)S(1)} %get-tuple-element.8, bf16[32,128,1,48]{1,3,0,2:T(8,128)(2,1)S(1)} %copy-done.10, bf16[31,128,1,48]{1,3,0,2:T(8,128)(2,1)} %slice.79, bf16[1,128,1,48]{1,3,0,2:T(8,128)(2,1)} %bitcast.15, ...), kind=kOutput, calls=%fused_computation.6 | convolution fusion | flops 106164224 | bytes 9601024 | tf_op jit(solution)/shard_map/nihd,njhd->nhij/dot_general | solution.py:85
  135.7 2.0 copy-done.1
  137.7 5.0 %fusion.4 = bf16[16,128,256]{2,0,1:T(8,128)(2,1)} fusion(f32[32,128,256]{2,1,0:T(8,128)S(1)} %subtract_multiply_fusion, s32[32]{0:T(128)S(1)} %copy-done.27), kind=kOutput, calls=%fused_computation.10 | convolution fusion | flops 201851392 | bytes 5243008 | tf_op jit(solution)/shard_map/nt,nhij->thij/dot_general | solution.py:174
  142.7 3.0 %fusion.16 = f32[32,48,256]{2,1,0:T(8,128)S(1)} fusion(bf16[32,128,48]{1,0,2:T(8,128)(2,1)S(1)} %copy-done.16, f32[32,128,256]{2,1,0:T(8,128)} %get-tuple-element.9, f32[32,128]{1,0:T(8,128)S(1)} %get-tuple-element.8), kind=kOutput, calls=%fused_computation.32 | convolution fusion | flops 102760448 | bytes 6176768 | tf_op jit(solution)/shard_map/nhij,nihd->njhd/dot_general | solution.py:98
  150.5 7.2 %all-to-all-start.5 = ((bf16[16,256,48]{1,2,0:T(8,128)(2,1)}), bf16[16,256,48]{1,2,0:T(8,128)(2,1)}, u32[]{:S(2)}, u32[]{:S(2)}) async-start(bf16[16,256,48]{1,2,0:T(8,128)(2,1)} %copy.117), calls=%async_computation.5 | async-start | bytes 786432 | tf_op jit(solution)/shard_map/all_to_all | solution.py:184
  159.0 2.8 convolution_multiply_fusion
  166.4 3.3 %all-to-all-done.5 = bf16[16,256,48]{1,2,0:T(8,128)(2,1)} async-done(((bf16[16,256,48]{1,2,0:T(8,128)(2,1)}), bf16[16,256,48]{1,2,0:T(8,128)(2,1)}, u32[]{:S(2)}, u32[]{:S(2)}) %all-to-all-start.5) | async-done | bytes 393248 | tf_op jit(solution)/shard_map/all_to_all | solution.py:184
  169.7 5.9 %all-to-all-start.7 = ((bf16[16,256,48]{1,2,0:T(8,128)(2,1)}), bf16[16,256,48]{1,2,0:T(8,128)(2,1)}, u32[]{:S(2)}, u32[]{:S(2)}) async-start(bf16[16,256,48]{1,2,0:T(8,128)(2,1)} %bitcast.172), calls=%async_computation.7 | async-start | bytes 786432 | tf_op jit(solution)/shard_map/all_to_all | solution.py:186
  178.7 9.1 %all-to-all-done.7 = bf16[16,256,48]{1,2,0:T(8,128)(2,1)} async-done(((bf16[16,256,48]{1,2,0:T(8,128)(2,1)}), bf16[16,256,48]{1,2,0:T(8,128)(2,1)}, u32[]{:S(2)}, u32[]{:S(2)}) %all-to-all-start.7) | async-done | bytes 393248 | tf_op jit(solution)/shard_map/all_to_all | solution.py:186
  187.8 5.3 %all-to-all-start.6 = ((bf16[16,256,48]{1,2,0:T(8,128)(2,1)}), bf16[16,256,48]{1,2,0:T(8,128)(2,1)S(1)}, u32[]{:S(2)}, u32[]{:S(2)}) async-start(bf16[16,256,48]{1,2,0:T(8,128)(2,1)} %bitcast.159), calls=%async_computation.6 | async-start | bytes 786432 | tf_op jit(solution)/shard_map/all_to_all | solution.py:185
  193.1 3.3 %fusion.12 = f32[32,128,1,48]{1,3,0,2:T(8,128)S(1)} fusion(bf16[32,128,1,48]{1,3,0,2:T(8,128)(2,1)S(1)} %copy-done.11, bf16[31,128,1,48]{1,3,0,2:T(8,128)(2,1)S(1)} %copy-done.18, bf16[1,128,1,48]{1,3,0,2:T(8,128)(2,1)} %bitcast.15, f32[32,128,256]{2,1,0:T(8,128)} %get-tuple-element.9, f32[32,128]{1,0:T(8,128)S(1)} %get-tuple-element.8), kind=kOutput, calls=%fused_computation.27 | convolution fusion | flops 105512960 | bytes 5783552 | tf_op jit(solution)/shard_map/nhij,njhd->nihd/dot_general | solution.py:81
  197.8 2.5 fusion.35
  200.3 5.0 %all-to-all-done.6 = bf16[16,256,48]{1,2,0:T(8,128)(2,1)S(1)} async-done(((bf16[16,256,48]{1,2,0:T(8,128)(2,1)}), bf16[16,256,48]{1,2,0:T(8,128)(2,1)S(1)}, u32[]{:S(2)}, u32[]{:S(2)}) %all-to-all-start.6) | async-done | bytes 393248 | tf_op jit(solution)/shard_map/all_to_all | solution.py:185
  205.3 5.3 %all-to-all-start.8 = ((bf16[16,256,48]{1,2,0:T(8,128)(2,1)}), bf16[16,256,48]{1,2,0:T(8,128)(2,1)S(1)}, u32[]{:S(2)}, u32[]{:S(2)}) async-start(bf16[16,256,48]{1,2,0:T(8,128)(2,1)} %fusion.35), calls=%async_computation.8 | async-start | bytes 786432 | tf_op jit(solution)/shard_map/all_to_all | solution.py:187
  210.5 2.0 fusion.67
  215.3 7.3 %all-to-all-done.8 = bf16[16,256,48]{1,2,0:T(8,128)(2,1)S(1)} async-done(((bf16[16,256,48]{1,2,0:T(8,128)(2,1)}), bf16[16,256,48]{1,2,0:T(8,128)(2,1)S(1)}, u32[]{:S(2)}, u32[]{:S(2)}) %all-to-all-start.8) | async-done | bytes 393248 | tf_op jit(solution)/shard_map/all_to_all | solution.py:187
  224.4 44.8 %all-gather.3.cloned.1.call-done = bf16[256,128,256]{2,0,1:T(8,128)(2,1)} async-done(((bf16[16,128,256]{2,0,1:T(8,128)(2,1)}), bf16[256,128,256]{2,0,1:T(8,128)(2,1)}) %all-gather.3.cloned.1.call-update) | async-done | bytes 16777232 | tf_op jit(solution)/shard_map/all_gather | solution.py:177
  269.1 8.8 %reduce.8 = bf16[16,128,256]{2,0,1:T(8,128)(2,1)S(1)} reduce(bf16[16,16,128,256]{3,1,0,2:T(8,128)(2,1)} %bitcast.162, bf16[]{:T(256)} %constant.39.clone.1), dimensions={0}, to_apply=%region_10.11 | reduce | flops 7864320 | bytes 17825794 | tf_op jit(solution)/shard_map/reduce_sum | solution.py:177
  278.3 2.5 copy.131
  (140 shorter events, 53.9 us)
Async XLA Ops:
  7.2 32.2 %copy-start = (bf16[768,768]{1,0:T(8,128)(2,1)S(1)}, bf16[768,768]{1,0:T(8,128)(2,1)}, u32[]{:S(2)}) copy-start(bf16[768,768]{1,0:T(8,128)(2,1)} %param.16) | copy-start | bytes 3538948
  8.4 66.9 %copy-start.19 = (f32[256]{0:T(256)}, f32[256]{0:T(256)S(1)}, u32[]{:S(2)}) copy-start(f32[256]{0:T(256)S(1)} %broadcast_multiply_fusion.2) | copy-start | bytes 3076
  9.7 12.3 %copy-start.3 = (bf16[256,768]{1,0:T(8,128)(2,1)S(1)}, bf16[256,768]{1,0:T(8,128)(2,1)}, u32[]{:S(2)}) copy-start(bf16[256,768]{1,0:T(8,128)(2,1)} %param.11) | copy-start | bytes 1179652
  9.7 12.3 %copy-start.15 = (bf16[768,768]{1,0:T(8,128)(2,1)S(1)}, bf16[768,768]{1,0:T(8,128)(2,1)}, u32[]{:S(2)}) copy-start(bf16[768,768]{1,0:T(8,128)(2,1)} %param.13) | copy-start | bytes 3538948
  9.7 65.6 %copy-start.23 = (f32[256]{0:T(256)}, f32[256]{0:T(256)S(1)}, u32[]{:S(2)}) copy-start(f32[256]{0:T(256)S(1)} %add_rsqrt_fusion) | copy-start | bytes 3076
  10.5 64.8 %copy-start.21 = (f32[768]{0:T(1024)}, f32[768]{0:T(1024)S(1)}, u32[]{:S(2)}) copy-start(f32[768]{0:T(1024)S(1)} %convert_element_type.153) | copy-start | bytes 9220
  13.4 20.5 %all-to-all-start = ((bf16[256,16,48]{0,2,1:T(8,128)(2,1)}), bf16[256,16,48]{0,2,1:T(8,128)(2,1)S(1)}, u32[]{:S(2)}, u32[]{:S(2)}) async-start(bf16[256,16,48]{0,2,1:T(8,128)(2,1)} %bitcast), calls=%async_computation | async-start | bytes 786432 | tf_op jit(solution)/shard_map/all_to_all | solution.py:145
  33.8 17.6 %all-to-all-start.1 = ((bf16[256,16,48]{0,2,1:T(8,128)(2,1)}), bf16[256,16,48]{0,2,1:T(8,128)(2,1)S(1)}, u32[]{:S(2)}, u32[]{:S(2)}) async-start(bf16[256,16,48]{0,2,1:T(8,128)(2,1)} %bitcast.6), calls=%async_computation.1 | async-start | bytes 786432 | tf_op jit(solution)/shard_map/all_to_all | solution.py:144
  39.4 17.5 %copy-start.17 = (bf16[256,768]{1,0:T(8,128)(2,1)S(1)}, bf16[256,768]{1,0:T(8,128)(2,1)}, u32[]{:S(2)}) copy-start(bf16[256,768]{1,0:T(8,128)(2,1)} %param.21) | copy-start | bytes 1179652
  51.5 23.6 %copy-start.28 = (s32[16]{0:T(128)S(1)}, s32[16]{0:T(128)}, u32[]{:S(2)}) copy-start(s32[16]{0:T(128)} %param.19) | copy-start | bytes 196
  51.5 17.6 %all-to-all-start.3 = ((bf16[256,16,48]{0,2,1:T(8,128)(2,1)}), bf16[256,16,48]{0,2,1:T(8,128)(2,1)S(1)}, u32[]{:S(2)}, u32[]{:S(2)}) async-start(bf16[256,16,48]{0,2,1:T(8,128)(2,1)} %bitcast.11), calls=%async_computation.3 | async-start | bytes 786432 | tf_op jit(solution)/shard_map/all_to_all | solution.py:147
  59.6 15.5 %copy-start.26 = (s32[32]{0:T(128)}, s32[32]{0:T(128)S(1)}, u32[]{:S(2)}) copy-start(s32[32]{0:T(128)S(1)} %add_add_fusion) | copy-start | bytes 388
  69.0 17.4 %all-to-all-start.2 = ((bf16[256,16,48]{0,2,1:T(8,128)(2,1)}), bf16[256,16,48]{0,2,1:T(8,128)(2,1)S(1)}, u32[]{:S(2)}, u32[]{:S(2)}) async-start(bf16[256,16,48]{0,2,1:T(8,128)(2,1)} %bitcast.10), calls=%async_computation.2 | async-start | bytes 786432 | tf_op jit(solution)/shard_map/all_to_all | solution.py:148
  75.3 16.5 %copy-start.25 = (s32[16]{0:T(128)}, s32[16]{0:T(128)S(1)}, u32[]{:S(2)}) copy-start(s32[16]{0:T(128)S(1)} %reduce.9) | copy-start | bytes 196
  86.5 16.2 %copy-start.5 = (bf16[256,16,48]{0,2,1:T(8,128)(2,1)}, bf16[256,16,48]{0,2,1:T(8,128)(2,1)S(1)}, u32[]{:S(2)}) copy-start(bf16[256,16,48]{0,2,1:T(8,128)(2,1)S(1)} %all-to-all-done.2) | copy-start | bytes 1179652
  86.5 24.3 %all-to-all-start.4 = ((bf16[256,16,48]{0,2,1:T(8,128)(2,1)}), bf16[256,16,48]{0,2,1:T(8,128)(2,1)S(1)}, u32[]{:S(2)}, u32[]{:S(2)}) async-start(bf16[256,16,48]{0,2,1:T(8,128)(2,1)} %bitcast.171), calls=%async_computation.4 | async-start | bytes 786432 | tf_op jit(solution)/shard_map/all_to_all | solution.py:146
  91.7 177.4 %all-gather.3.cloned.1.call-start = ((), (), s32[]{:S(2)}) async-start(), calls=%async_computation.9 | async-start | bytes 17825792 | tf_op jit(solution)/shard_map/all_gather | solution.py:177
  98.6 19.3 %collective-permute-start = (bf16[128,48]{0,1:T(8,128)(2,1)S(1)}, bf16[128,48]{0,1:T(8,128)(2,1)}, u32[]{:S(2)}, u32[]{:S(2)}) collective-permute-start(bf16[128,48]{0,1:T(8,128)(2,1)S(1)} %slice.76), channel_id=1, source_target_pairs={{0,16},{16,32},{32,48},{48,64},{64,80},{80,96},{96,112},{112,128},... | collective-permute-start | bytes 36872 | tf_op jit(solution)/shard_map/ppermute | solution.py:14
  114.4 15.7 %collective-permute-start.1 = (bf16[128,48]{0,1:T(8,128)(2,1)}, bf16[128,48]{0,1:T(8,128)(2,1)}, u32[]{:S(2)}, u32[]{:S(2)}) collective-permute-start(bf16[128,48]{0,1:T(8,128)(2,1)} %slice.78), channel_id=1, source_target_pairs={{0,16},{16,32},{32,48},{48,64},{64,80},{80,96},{96,112},{112,128},... | collective-permute-start | bytes 36872 | tf_op jit(solution)/shard_map/ppermute | solution.py:14
  117.9 12.2 %copy-start.10 = (bf16[32,128,1,48]{1,3,0,2:T(8,128)(2,1)S(1)}, bf16[32,128,1,48]{1,3,0,2:T(8,128)(2,1)}, u32[]{:S(2)}) copy-start(bf16[32,128,1,48]{1,3,0,2:T(8,128)(2,1)} %copy-done.9) | copy-start | bytes 1179652
  117.9 12.2 %copy-start.16 = (bf16[32,128,48]{1,0,2:T(8,128)(2,1)S(1)}, bf16[32,128,48]{1,0,2:T(8,128)(2,1)}, u32[]{:S(2)}) copy-start(bf16[32,128,48]{1,0,2:T(8,128)(2,1)} %reshape.273) | copy-start | bytes 1179652
  146.5 18.4 %collective-permute-start.3 = (bf16[128,48]{0,1:T(8,128)(2,1)}, bf16[128,48]{0,1:T(8,128)(2,1)}, u32[]{:S(2)}, u32[]{:S(2)}) collective-permute-start(bf16[128,48]{0,1:T(8,128)(2,1)} %fusion.49), channel_id=1, source_target_pairs={{16,0},{32,16},{48,32},{64,48},{80,64},{96,80},{112,96},{128,112},... | collective-permute-start | bytes 36872 | tf_op jit(solution)/shard_map/ppermute | solution.py:14
  150.5 19.2 %all-to-all-start.5 = ((bf16[16,256,48]{1,2,0:T(8,128)(2,1)}), bf16[16,256,48]{1,2,0:T(8,128)(2,1)}, u32[]{:S(2)}, u32[]{:S(2)}) async-start(bf16[16,256,48]{1,2,0:T(8,128)(2,1)} %copy.117), calls=%async_computation.5 | async-start | bytes 786432 | tf_op jit(solution)/shard_map/all_to_all | solution.py:184
  163.6 13.6 %collective-permute-start.2 = (bf16[128,48]{0,1:T(8,128)(2,1)}, bf16[128,48]{0,1:T(8,128)(2,1)}, u32[]{:S(2)}, u32[]{:S(2)}) collective-permute-start(bf16[128,48]{0,1:T(8,128)(2,1)} %fusion.48), channel_id=1, source_target_pairs={{16,0},{32,16},{48,32},{64,48},{80,64},{96,80},{112,96},{128,112},... | collective-permute-start | bytes 36872 | tf_op jit(solution)/shard_map/ppermute | solution.py:14
  169.7 18.1 %all-to-all-start.7 = ((bf16[16,256,48]{1,2,0:T(8,128)(2,1)}), bf16[16,256,48]{1,2,0:T(8,128)(2,1)}, u32[]{:S(2)}, u32[]{:S(2)}) async-start(bf16[16,256,48]{1,2,0:T(8,128)(2,1)} %bitcast.172), calls=%async_computation.7 | async-start | bytes 786432 | tf_op jit(solution)/shard_map/all_to_all | solution.py:186
  176.9 16.2 %copy-start.11 = (bf16[32,128,1,48]{1,3,0,2:T(8,128)(2,1)S(1)}, bf16[32,128,1,48]{1,3,0,2:T(8,128)(2,1)}, u32[]{:S(2)}) copy-start(bf16[32,128,1,48]{1,3,0,2:T(8,128)(2,1)} %copy-done.9) | copy-start | bytes 1179652
  176.9 16.2 %copy-start.18 = (bf16[31,128,1,48]{1,3,0,2:T(8,128)(2,1)S(1)}, bf16[31,128,1,48]{1,3,0,2:T(8,128)(2,1)}, u32[]{:S(2)}) copy-start(bf16[31,128,1,48]{1,3,0,2:T(8,128)(2,1)} %slice.79) | copy-start | bytes 1142788
  187.8 17.5 %all-to-all-start.6 = ((bf16[16,256,48]{1,2,0:T(8,128)(2,1)}), bf16[16,256,48]{1,2,0:T(8,128)(2,1)S(1)}, u32[]{:S(2)}, u32[]{:S(2)}) async-start(bf16[16,256,48]{1,2,0:T(8,128)(2,1)} %bitcast.159), calls=%async_computation.6 | async-start | bytes 786432 | tf_op jit(solution)/shard_map/all_to_all | solution.py:185
  205.3 17.4 %all-to-all-start.8 = ((bf16[16,256,48]{1,2,0:T(8,128)(2,1)}), bf16[16,256,48]{1,2,0:T(8,128)(2,1)S(1)}, u32[]{:S(2)}, u32[]{:S(2)}) async-start(bf16[16,256,48]{1,2,0:T(8,128)(2,1)} %fusion.35), calls=%async_computation.8 | async-start | bytes 786432 | tf_op jit(solution)/shard_map/all_to_all | solution.py:187
  213.1 9.5 %copy-start.20 = (f32[256]{0:T(256)S(1)}, f32[256]{0:T(256)}, u32[]{:S(2)}) copy-start(f32[256]{0:T(256)} %copy-done.19) | copy-start | bytes 3076
  213.1 9.5 %copy-start.22 = (f32[768]{0:T(1024)S(1)}, f32[768]{0:T(1024)}, u32[]{:S(2)}) copy-start(f32[768]{0:T(1024)} %copy-done.21) | copy-start | bytes 9220
  213.1 9.5 %copy-start.24 = (f32[256]{0:T(256)S(1)}, f32[256]{0:T(256)}, u32[]{:S(2)}) copy-start(f32[256]{0:T(256)} %copy-done.23) | copy-start | bytes 3076
  (11 other events, 38.2 us)
Sparse Core Ops, SparseCore 0:
  142.8 126.2 all-gather.2
